TPU v7x, 256 devices: a whole 4x4x8 slice. The times are simulated.
256 devices in a mesh: blk: 128 (over z, x, y), rhs: 2 (over core).
Axes of the slice: x: 4, y: 4, z: 8, core: 2. Of those that a mesh axis runs over, the one named last changes fastest.
Arguments:
- right_side: float32 [1024, 128, 128], P('blk', 'rhs'), may hold values from -8.4 to 8.4
- diag_tiles: bfloat16 [1024, 128, 128], P('blk'), may hold values from -0.085 to 1.33, as said below
- cond_tiles: bfloat16 [1024, 8, 128, 128], P('blk', 'rhs'), may hold values from -0.046875 to 0.046875
- neighbour_blocks: int32 [1024, 8], P('blk'), may hold values from 0 to 1023, as said below
- precision_diag: float32 [1024, 128], P('blk'), may hold values from 0.5 to 2
- precond_tiles: bfloat16 [1024, 128, 128], P('blk'), may hold values from -0.08 to 2.08, as said below
Outputs:
- solution: float32 [1024, 128, 128], P('blk', 'rhs')
- residual: float32 [1024, 128, 128], P('blk', 'rhs')
Inputs may be any that keep to these rules, and one draw needn't show every extreme that they name: `neighbour_blocks`: device d holds blocks 8 * d to 8 * d + 7. No block names itself; every block names exactly 7 blocks held by other devices, and the lists of one device's blocks name blocks of any one other device at most 1 times in all, a bound that is reached. `diag_tiles`: each tile has a positive diagonal. `precond_tiles`: each tile is symmetric with a positive diagonal.
All inputs are finite; a program needn't handle non-finite values.
Results may differ from a plain program's by a relative error of at most 0.0003.
Values may be sent and summed in bfloat16 or wider, within the bound.
No kernel may reach another device: no remote copies, remote signals or barrier semaphores. Data moves between devices by JAX's collectives and lax.ppermute only.
A program may use at most 128 MiB of HBM per device.

v0:
```python
import jax
import jax.numpy as jnp
import numpy as np
from jax import lax
from jax.experimental import pallas as pl
from jax.experimental.pallas import tpu as pltpu
from jax.sharding import Mesh, PartitionSpec as P

ITERS = 3
DIMS = (8, 4, 4)
LANES = 128
COLS = 8
SHARE = 8
GROUPS = 3
EXTRA = (GROUPS + 1) * COLS
BUFFERS = 8
LOW_EXP = -100.0
F32, BF16, I16, I32 = jnp.float32, jnp.bfloat16, jnp.int16, jnp.int32
VMEM_LIMIT = 12 * 1024 * 1024
STREAM_LIMIT = 36 * 1024 * 1024


def spread(column):
    return jnp.broadcast_to(column, (column.shape[0], LANES))


def split_rows(values):
    lead = values.astype(BF16).astype(F32)
    return jnp.concatenate([lead, values - lead], axis=0).astype(BF16)


def join_rows(values):
    return values[:COLS] + values[COLS:]


def group_ranges(blocks):
    pairs = blocks // 2
    cuts = [2 * (pairs * part // GROUPS) for part in range(GROUPS + 1)]
    return list(zip(cuts[:-1], cuts[1:]))


def exponents(tops):
    exps = jnp.floor(jnp.log2(jnp.maximum(tops, 1e-35) * 1.0025)) + 1.0
    return jnp.clip(exps, LOW_EXP, 126.0)


def encode(read, blocks, partial, write):
    tail = []
    for low, high in group_ranges(blocks):
        tops = jnp.abs(read(low))
        for block in range(low + 1, high):
            tops = jnp.maximum(tops, jnp.abs(read(block)))
        exps = exponents(tops)
        tail.append(exps)
        scale = jnp.exp2(15.0 - exps)
        for block in range(low, high, 2):
            pair = jnp.concatenate([read(block) * scale, read(block + 1) * scale], axis=0)
            write(block * COLS, jnp.round(pair).astype(I32).astype(I16))
    total = spread(jnp.sum(partial, axis=1, keepdims=True))
    exps = exponents(jnp.abs(total))
    scaled = total * (jnp.exp2(15.0 - exps) * 0.5)
    first = jnp.round(scaled)
    second = jnp.round((scaled - first) * 32768.0)
    lane = lax.broadcasted_iota(I32, (COLS, LANES), 1)
    tail.append(jnp.where(lane == 0, exps, jnp.where(lane == 1, first, second)))
    for part in range(0, GROUPS + 1, 2):
        rows = jnp.concatenate(tail[part : part + 2], axis=0)
        write((blocks + part) * COLS, rows.astype(I32).astype(I16))


def widen(rows):
    return rows.astype(I32).astype(F32)


def decode_tail(rows):
    rows = widen(rows)
    scales = [jnp.exp2(rows[part * COLS : (part + 1) * COLS] - 15.0) for part in range(GROUPS)]
    tail = rows[GROUPS * COLS :]
    whole = tail[:, 1:2] + tail[:, 2:3] * (1.0 / 32768.0)
    total = spread(whole) * (jnp.exp2(spread(tail[:, 0:1]) - 15.0) * 2.0)
    return scales, total


def decode_blocks(read, scales, blocks, take):
    for scale, (low, high) in zip(scales, group_ranges(blocks)):
        for block in range(low, high, 2):
            values = widen(read(block * COLS))
            take(block, values[:COLS] * scale)
            take(block + 1, values[COLS:] * scale)


def start_kernel(shaped_ref, residual_ref, code_ref):
    blocks = shaped_ref.shape[0]
    partial = jnp.zeros((COLS, LANES), F32)
    for block in range(blocks):
        partial = partial + shaped_ref[block] * residual_ref[block]

    def write(row, value):
        code_ref[row : row + 2 * COLS, :] = value

    encode(lambda block: shaped_ref[block], blocks, partial, write)


def factor_kernel(first, last, peers, *refs):
    refs = list(refs)
    near_ref, me_ref, code_ref, shaped_ref, precision_ref, tiles_ref = refs[:6]
    refs = refs[6:]
    if not first:
        old_field_ref, old_direction_ref, old_gamma_ref = refs[:3]
        refs = refs[3:]
    out_ref, own_ref, direction_ref, gamma_ref = refs[:4]
    field_ref, running_ref, partial_ref, held_ref, semaphores = refs[4:]
    blocks = shaped_ref.shape[0]
    step_blocks = SHARE
    steps = blocks // step_blocks
    half = step_blocks // 2
    slots = 4
    buffers = held_ref.shape[0]

    def fetch(step):
        buffer = lax.rem(step, buffers)
        return pltpu.make_async_copy(tiles_ref.at[step], held_ref.at[buffer], semaphores.at[buffer])

    for step in range(min(buffers, steps)):
        fetch(step).start()

    def prologue():
        gamma = jnp.zeros((COLS, LANES), F32)
        for peer in range(peers):
            gamma = gamma + decode_tail(code_ref[peer, blocks * COLS :, :])[1]
        gamma_ref[...] = gamma
        if not first:
            beta = gamma / old_gamma_ref[...]

        def take(peer, carry):
            scales, unused = decode_tail(code_ref[peer, blocks * COLS :, :])

            def keep(block, values):
                place = peer * blocks + block
                if not first:
                    values = values + beta * join_rows(old_field_ref[place].astype(F32))
                field_ref[place] = split_rows(values)
                running_ref[place] = jnp.zeros((COLS, LANES), F32)

            def read(row):
                return code_ref[peer, row : row + 2 * COLS, :]

            decode_blocks(read, scales, blocks, keep)
            return carry

        lax.fori_loop(0, peers, take, 0)
        for block in range(blocks):
            values = shaped_ref[block]
            if not first:
                values = values + beta * old_direction_ref[block]
            direction_ref[block] = values
        partial_ref[...] = jnp.zeros_like(partial_ref)

    def work(step, at):
        def tile_row(inner):
            parts = [
                held_ref[at, core, inner * slots + slot]
                for core in range(2)
                for slot in range(slots)
            ]
            parts.append(held_ref[at, inner // half, slots * step_blocks + inner % half])
            return jnp.concatenate(parts, axis=1)

        partial = partial_ref[...]
        kept = []
        for inner in range(step_blocks):
            block = step * step_blocks + inner
            places = [near_ref[block * 2 * slots + k] for k in range(2 * slots)]
            left = [field_ref[place] for place in places] + [split_rows(direction_ref[block])]
            summed = join_rows(
                lax.dot_general(
                    jnp.concatenate(left, axis=1),
                    tile_row(inner),
                    (((1,), (1,)), ((), ())),
                    preferred_element_type=F32,
                )
            )
            weighted = precision_ref[pl.ds(block, 1), :] * summed
            partial = partial + weighted * summed
            kept.append((block, places, split_rows(weighted)))
        partial_ref[...] = partial
        for inner, (block, places, weighted) in enumerate(kept):
            pieces = join_rows(
                jnp.dot(weighted, tile_row(inner), preferred_element_type=F32)
            )
            own_ref[block] = pieces[:, 2 * slots * LANES :]
            for k, place in enumerate(places):
                running_ref[place] = running_ref[place] + pieces[:, k * LANES : (k + 1) * LANES]

    def epilogue():
        me = me_ref[0]
        for block in range(blocks):
            own_ref[block] = own_ref[block] + running_ref[me * blocks + block]

        def give(peer, carry):
            def write(row, value):
                out_ref[peer, row : row + 2 * COLS, :] = value

            encode(lambda block: running_ref[peer * blocks + block], blocks, partial_ref[...], write)
            return carry

        lax.fori_loop(0, peers, give, 0)

    def loop(step, carry):
        fetch(step).wait()
        work(step, lax.rem(step, buffers))

        @pl.when(step + buffers < steps)
        def refill():
            fetch(step + buffers).start()

        return carry

    prologue()
    lax.fori_loop(0, steps, loop, 0)
    epilogue()


def update_kernel(last, peers, *refs):
    refs = list(refs)
    me_ref, code_ref, own_ref, residual_ref, solution_ref, direction_ref, gamma_ref = refs[:7]
    refs = refs[7:]
    if last:
        out_ref, new_residual_ref, new_solution_ref, image_ref = refs
    else:
        precond_ref, new_residual_ref, new_solution_ref, shaped_ref, out_ref, image_ref = refs
    blocks = own_ref.shape[0]
    me = me_ref[0]
    for block in range(blocks):
        image_ref[block] = own_ref[block]

    def take(peer, bottom):
        scales, total = decode_tail(code_ref[peer, blocks * COLS :, :])
        scales = [jnp.where(peer == me, 0.0, scale) for scale in scales]

        def read(row):
            return code_ref[peer, row : row + 2 * COLS, :]

        def add(block, values):
            image_ref[block] = image_ref[block] + values

        decode_blocks(read, scales, blocks, add)
        return bottom + total

    bottom = lax.fori_loop(0, peers, take, jnp.zeros((COLS, LANES), F32))
    alpha = gamma_ref[...] / bottom
    partial = jnp.zeros((COLS, LANES), F32)
    for block in range(blocks):
        new_solution_ref[block] = solution_ref[block] + alpha * direction_ref[block]
        residual = residual_ref[block] - alpha * image_ref[block]
        new_residual_ref[block] = residual
        if not last:
            shaped = join_rows(
                jnp.dot(split_rows(residual), precond_ref[block], preferred_element_type=F32)
            )
            shaped_ref[block] = shaped
            partial = partial + residual * shaped
    if not last:

        def write(row, value):
            out_ref[row : row + 2 * COLS, :] = value

        encode(lambda block: shaped_ref[block], blocks, partial, write)
    else:
        for plane in range(blocks // SHARE):
            for part, ref in enumerate((new_solution_ref, new_residual_ref)):
                first = plane * SHARE
                tops = jnp.abs(ref[first])
                for inner in range(1, SHARE):
                    tops = jnp.maximum(tops, jnp.abs(ref[first + inner]))
                exps = exponents(tops)
                scale = jnp.exp2(15.0 - exps)
                for inner in range(0, SHARE, 2):
                    pair = jnp.concatenate(
                        [ref[first + inner] * scale, ref[first + inner + 1] * scale], axis=0
                    )
                    row = (part * SHARE + inner) * COLS
                    out_ref[plane, row : row + 2 * COLS, :] = jnp.round(pair).astype(I32).astype(I16)
                kept = exps if part == 0 else jnp.concatenate([kept, exps], axis=0)
            out_ref[plane, 2 * SHARE * COLS :, :] = kept.astype(I32).astype(I16)


def finish_kernel(code_ref, solution_ref, residual_ref):
    for plane in range(code_ref.shape[0]):
        scales = jnp.exp2(widen(code_ref[plane, 2 * SHARE * COLS :, :]) - 15.0)
        for part, ref in enumerate((solution_ref, residual_ref)):
            scale = scales[part * COLS : (part + 1) * COLS]
            for inner in range(0, SHARE, 2):
                row = (part * SHARE + inner) * COLS
                values = widen(code_ref[plane, row : row + 2 * COLS, :])
                columns = slice(plane * COLS, (plane + 1) * COLS)
                ref[inner, columns, :] = values[:COLS] * scale
                ref[inner + 1, columns, :] = values[COLS:] * scale


WHOLE = pl.BlockSpec(memory_space=pltpu.VMEM)
SCALARS = pl.BlockSpec(memory_space=pltpu.SMEM)
PARAMS = pltpu.CompilerParams(vmem_limit_bytes=VMEM_LIMIT)


def start_call(shaped, residual):
    blocks = shaped.shape[0]
    return pl.pallas_call(
        start_kernel,
        out_shape=jax.ShapeDtypeStruct((blocks * COLS + EXTRA, LANES), I16),
        in_specs=[WHOLE, WHOLE],
        out_specs=WHOLE,
        compiler_params=PARAMS,
        name="start",
    )(shaped, residual)


def factor_call(first, last, near, me, codes, shaped, precision, tiles, state):
    peers = codes.shape[0]
    blocks = shaped.shape[0]
    field = (peers * blocks, 2 * COLS, LANES)

    arguments = (near, me, codes, shaped, precision, tiles, *state)
    outs = [
        (codes.shape, I16),
        (shaped.shape, F32),
        (shaped.shape, F32),
        ((COLS, LANES), F32),
    ]
    scratch = [
        pltpu.VMEM((peers * blocks, COLS, LANES), F32),
        pltpu.VMEM((COLS, LANES), F32),
        pltpu.VMEM((BUFFERS,) + tiles.shape[1:], BF16),
        pltpu.SemaphoreType.DMA((BUFFERS,)),
    ]
    if last:
        scratch = [pltpu.VMEM(field, BF16)] + scratch
    else:
        outs.append((field, BF16))
    return pl.pallas_call(
        lambda *refs: factor_kernel(first, last, peers, *refs),
        out_shape=[jax.ShapeDtypeStruct(*out) for out in outs],
        in_specs=[SCALARS] * 2
        + [WHOLE] * 3
        + [pl.BlockSpec(memory_space=pl.ANY)]
        + [WHOLE] * (len(arguments) - 6),
        out_specs=[WHOLE] * len(outs),
        scratch_shapes=scratch,
        compiler_params=pltpu.CompilerParams(vmem_limit_bytes=STREAM_LIMIT),
        name="factor",
    )(*arguments)


def update_call(last, me, codes, own, residual, answer, direction, gamma, precond):
    shape = jax.ShapeDtypeStruct(own.shape, F32)
    arguments = [me, codes, own, residual, answer, direction, gamma]
    if last:
        rows = 2 * SHARE * COLS + 2 * COLS
        outs = [jax.ShapeDtypeStruct((own.shape[0] // SHARE, rows, LANES), I16)]
        scratch = [pltpu.VMEM(own.shape, F32)] * 3
    else:
        outs = [shape, shape, shape, jax.ShapeDtypeStruct(codes.shape[1:], I16)]
        scratch = [pltpu.VMEM(own.shape, F32)]
        arguments.append(precond)
    in_specs = [SCALARS] + [WHOLE] * (len(arguments) - 1)
    return pl.pallas_call(
        lambda *refs: update_kernel(last, codes.shape[0], *refs),
        out_shape=outs,
        in_specs=in_specs,
        out_specs=[WHOLE] * len(outs),
        scratch_shapes=scratch,
        compiler_params=PARAMS,
        name="update",
    )(*arguments)


def finish_call(codes):
    shape = jax.ShapeDtypeStruct((SHARE, codes.shape[0] * COLS, LANES), F32)
    return pl.pallas_call(
        finish_kernel,
        out_shape=[shape, shape],
        in_specs=[WHOLE],
        out_specs=[WHOLE, WHOLE],
        compiler_params=PARAMS,
        name="finish",
    )(codes)


def local(right_side, diag_tiles, cond_tiles, neighbour_blocks, precision_diag, precond_tiles):
    depth, wide, high = (lax.axis_size(name) for name in ("z", "x", "y"))
    peers = wide * high
    here = right_side.shape[0]
    blocks = depth * here
    core = lax.axis_index("c")
    me = (lax.axis_index("x") * high + lax.axis_index("y")).astype(I32).reshape(1)
    half = here // 2

    own_diag = jnp.where(core == 0, diag_tiles[:half], diag_tiles[half:])
    mine = jnp.concatenate([cond_tiles.reshape(-1, LANES, LANES), own_diag], axis=0)
    tiles = lax.all_gather(mine, ("z", "c"), axis=0, tiled=False)
    tiles = tiles.reshape((depth, 2) + mine.shape)
    own_precond = lax.dynamic_slice_in_dim(precond_tiles, core * half, half, 0)

    wide_precond = precond_tiles.astype(F32)
    shaped = jnp.einsum("lts,lcs->lct", wide_precond, right_side, precision=lax.Precision.HIGHEST)
    near = jnp.pad(neighbour_blocks.astype(F32), ((0, 0), (0, LANES - neighbour_blocks.shape[1])))
    facts = jnp.concatenate([precision_diag, near], axis=0)
    facts = jnp.broadcast_to(facts[None], (depth,) + facts.shape)

    def by_column(values):
        values = values.reshape(here, depth, COLS, LANES).transpose(1, 0, 2, 3)
        return values.reshape(depth, here * COLS, LANES)

    sent = jnp.concatenate([by_column(right_side), by_column(shaped), facts], axis=1)
    came = lax.all_to_all(sent, "z", split_axis=0, concat_axis=0, tiled=True)
    rows = here * COLS
    residual = came[:, :rows].reshape(blocks, COLS, LANES)
    shaped = came[:, rows : 2 * rows].reshape(blocks, COLS, LANES)
    precision = came[:, 2 * rows : 2 * rows + here].reshape(blocks, LANES)
    near = came[:, 2 * rows + here :, : neighbour_blocks.shape[1]].astype(I32).reshape(-1)
    plane = near // (peers * here)
    near = (near // here) % peers * blocks + plane * here + near % here

    answer = jnp.zeros_like(residual)
    codes = start_call(shaped, residual)
    state = ()
    for iteration in range(ITERS):
        last = iteration + 1 == ITERS
        arrived = lax.all_gather(codes, ("x", "y"), axis=0, tiled=False)
        if iteration == 0:
            arrived, near, precision, tiles, own_precond = lax.optimization_barrier(
                (arrived, near, precision, tiles, own_precond)
            )
            precond = lax.all_gather(own_precond, ("z", "c"), axis=0, tiled=True)
        leaving, own, direction, gamma, *field = factor_call(
            iteration == 0, last, near, me, arrived, shaped, precision, tiles, state
        )
        terms = lax.all_to_all(leaving, ("x", "y"), split_axis=0, concat_axis=0, tiled=True)
        results = update_call(
            last, me, terms, own, residual, answer, direction, gamma, precond
        )
        if not last:
            residual, answer, shaped, codes = results
            state = (field[0], direction, gamma)

    codes = lax.all_to_all(results[0], "z", split_axis=0, concat_axis=0, tiled=True)
    answer, residual = finish_call(codes)
    return answer, residual


def solution(mesh, dims=DIMS):
    grid = Mesh(np.asarray(mesh.devices).reshape(dims + (2,)), ("z", "x", "y", "c"))
    blk = ("z", "x", "y")
    return jax.shard_map(
        local,
        mesh=grid,
        in_specs=(P(blk, "c", None), P(blk), P(blk, "c"), P(blk), P(blk), P(blk)),
        out_specs=(P(blk, "c", None), P(blk, "c", None)),
        check_vma=False,
    )
```

profile of v0, /device:TPU:2, one launch (start us, length us, event | category | flops | bytes accessed | tf_op | source)
XLA Modules:
  0.0 343.2 jit_solution(14719155527565150687)
XLA Ops:
  7.2 0.0 copy-start
  7.2 0.0 copy-start.8
  7.2 0.0 copy-start.9
  7.2 0.0 copy-start.7
  7.2 0.0 all-gather.12.cloned.1.call-start
  7.3 1.1 slice_select_fusion
  8.3 2.4 pad_maximum_fusion
  10.7 0.0 all-gather.12.cloned.1.call-update
  10.7 0.0 copy-done.8
  10.7 0.0 copy-done.9
  10.8 0.0 copy-done
  10.8 0.0 copy-done.7
  10.8 0.6 convolution_bitcast_fusion
  11.5 0.9 pad_maximum_fusion.1
  12.3 8.5 %all-to-all-start = ((f32[8,144,128]{2,1,0:T(8,128)}), f32[8,144,128]{2,1,0:T(8,128)S(1)}, u32[]{:S(2)}, u32[]{:S(2)}) async-start(f32[8,144,128]{2,1,0:T(8,128)} %pad_maximum_fusion.1), calls=%async_computation | async-start | bytes 1179648 | tf_op jit(solution)/shard_map/all_to_all | solution.py:415
  20.8 0.0 all-gather.10.cloned.1.call-start
  20.8 0.7 constant_dynamic-slice_fusion
  21.5 22.8 %all-to-all-done = f32[8,144,128]{2,1,0:T(8,128)S(1)} async-done(((f32[8,144,128]{2,1,0:T(8,128)}), f32[8,144,128]{2,1,0:T(8,128)S(1)}, u32[]{:S(2)}, u32[]{:S(2)}) %all-to-all-start) | async-done | bytes 589856 | tf_op jit(solution)/shard_map/all_to_all | solution.py:415
  44.3 0.1 reshape.45
  44.5 0.2 start.1
  44.7 28.2 %all-gather.13 = s16[8704,128]{1,0:T(8,128)(2,1)S(1)} all-gather(s16[544,128]{1,0:T(8,128)(2,1)S(1)} %start.1), channel_id=2, replica_groups=mesh['z'=8,'x'=4,'y'=4,'c'=2] {'x','y'}, dimensions={0}, use_global_device_ids=true | all-gather | bytes 2367488 | tf_op jit(solution)/shard_map/all_gather | solution.py:429
  72.8 54.6 %all-gather.12.cloned.1.call-done = bf16[576,128,128]{2,1,0:T(8,128)(2,1)} async-done(((bf16[36,128,128]{2,1,0:T(8,128)(2,1)}), bf16[576,128,128]{2,1,0:T(8,128)(2,1)}) %all-gather.12.cloned.1.call-update) | async-done | bytes 18874384 | tf_op jit(solution)/shard_map/all_gather | solution.py:400
  127.4 0.0 all-gather.10.cloned.1.call-update
  127.4 13.2 %factor.3 = (s16[16,544,128]{2,1,0:T(8,128)(2,1)S(1)}, f32[64,8,128]{2,1,0:T(8,128)S(1)}, f32[64,8,128]{2,1,0:T(8,128)S(1)}, f32[8,128]{1,0:T(8,128)S(1)}, bf16[1024,16,128]{2,1,0:T(8,128)(2,1)S(1)}) custom-call(s32[512]{0:T(512)S(1)} %fusion.3.refs_0_, s32[1]{0:T(128)} %bitcast.refs_1_.refs_0_, s16[16,544,128]{2,1,0:T(8,128)(2,1)S(1)} %bitcast.25, ...), custom_call_target="tpu_custom_call" | custom-call | tf_op jit(solution)/shard_map/factor/pallas_call | solution.py:340
  140.6 0.0 copy-start.3
  140.7 2.0 copy-done.3
  142.7 0.0 copy-start.5
  142.7 0.7 copy-done.5
  143.4 35.8 %all_to_all.25.refs_1_ = s16[16,544,128]{2,1,0:T(8,128)(2,1)S(1)} all-to-all(s16[16,544,128]{2,1,0:T(8,128)(2,1)S(1)} %get-tuple-element.33), channel_id=1, replica_groups=mesh['z'=8,'x'=4,'y'=4,'c'=2] {'x','y'}, dimensions={0} | all-to-all | bytes 4456448 | tf_op jit(solution)/shard_map/all_to_all | solution.py:438
  179.2 0.0 all-gather.10.cloned.1.call-done.refs_7_
  179.2 0.0 copy-start.1
  179.2 1.6 copy-done.1
  180.8 0.0 copy-start.6
  180.8 0.9 copy-done.6
  181.8 0.0 copy-start.4
  181.8 3.1 update.3
  184.9 25.5 %all-gather.14 = s16[8704,128]{1,0:T(8,128)(2,1)S(1)} all-gather(s16[544,128]{1,0:T(8,128)(2,1)S(1)} %get-tuple-element.38), channel_id=4, replica_groups=mesh['z'=8,'x'=4,'y'=4,'c'=2] {'x','y'}, dimensions={0}, use_global_device_ids=true | all-gather | bytes 2367488 | tf_op jit(solution)/shard_map/all_gather | solution.py:429
  210.4 0.0 copy-done.4
  210.4 13.5 %factor.4 = (s16[16,544,128]{2,1,0:T(8,128)(2,1)S(1)}, f32[64,8,128]{2,1,0:T(8,128)S(1)}, f32[64,8,128]{2,1,0:T(8,128)S(1)}, f32[8,128]{1,0:T(8,128)S(1)}, bf16[1024,16,128]{2,1,0:T(8,128)(2,1)S(1)}) custom-call(s32[512]{0:T(512)S(1)} %fusion.3.refs_0_, s32[1]{0:T(128)} %bitcast.refs_1_.refs_0_, s16[16,544,128]{2,1,0:T(8,128)(2,1)S(1)} %bitcast.27, ...), custom_call_target="tpu_custom_call" | custom-call | tf_op jit(solution)/shard_map/factor/pallas_call | solution.py:340
  223.9 0.0 copy-start.2
  223.9 29.3 %all_to_all.26.refs_1_ = s16[16,544,128]{2,1,0:T(8,128)(2,1)S(1)} all-to-all(s16[16,544,128]{2,1,0:T(8,128)(2,1)S(1)} %get-tuple-element.41), channel_id=1, replica_groups=mesh['z'=8,'x'=4,'y'=4,'c'=2] {'x','y'}, dimensions={0} | all-to-all | bytes 4456448 | tf_op jit(solution)/shard_map/all_to_all | solution.py:438
  253.2 0.0 copy-done.2
  253.3 3.1 update.4
  256.3 25.1 %all-gather.15 = s16[8704,128]{1,0:T(8,128)(2,1)S(1)} all-gather(s16[544,128]{1,0:T(8,128)(2,1)S(1)} %get-tuple-element.47), channel_id=5, replica_groups=mesh['z'=8,'x'=4,'y'=4,'c'=2] {'x','y'}, dimensions={0}, use_global_device_ids=true | all-gather | bytes 2367488 | tf_op jit(solution)/shard_map/all_gather | solution.py:429
  281.5 13.5 %factor.5 = (s16[16,544,128]{2,1,0:T(8,128)(2,1)S(1)}, f32[64,8,128]{2,1,0:T(8,128)S(1)}, f32[64,8,128]{2,1,0:T(8,128)S(1)}, f32[8,128]{1,0:T(8,128)S(1)}) custom-call(s32[512]{0:T(512)S(1)} %fusion.3.refs_0_, s32[1]{0:T(128)} %bitcast.refs_1_.refs_0_, s16[16,544,128]{2,1,0:T(8,128)(2,1)S(1)} %bitcast.26, f32[64,8,128]{2,1,0:T(8,128)S(1)} %get-tuple-element.48.refs_3_, ...), custom_call_target="tpu_custom_call" | custom-call | tf_op jit(solution)/shard_map/factor/pallas_call | solution.py:340
  295.0 22.9 %all_to_all.27.refs_1_ = s16[16,544,128]{2,1,0:T(8,128)(2,1)S(1)} all-to-all(s16[16,544,128]{2,1,0:T(8,128)(2,1)S(1)} %get-tuple-element.50), channel_id=1, replica_groups=mesh['z'=8,'x'=4,'y'=4,'c'=2] {'x','y'}, dimensions={0} | all-to-all | bytes 4456448 | tf_op jit(solution)/shard_map/all_to_all | solution.py:438
  317.9 2.5 update.5
  320.4 15.2 %all_to_all.28.code_ref = s16[8,144,128]{2,1,0:T(8,128)(2,1)S(1)} all-to-all(s16[8,144,128]{2,1,0:T(8,128)(2,1)S(1)} %update.5), channel_id=1, replica_groups=mesh['z'=8,'x'=4,'y'=4,'c'=2] {'z'}, dimensions={0} | all-to-all | bytes 589824 | tf_op jit(solution)/shard_map/all_to_all | solution.py:446
  335.5 0.9 finish.1
  (9 shorter events, 0.2 us)
Async XLA Ops:
  7.2 3.6 %copy-start = (f32[8,64,128]{2,1,0:T(8,128)S(1)}, f32[8,64,128]{2,1,0:T(8,128)}, u32[]{:S(2)}) copy-start(f32[8,64,128]{2,1,0:T(8,128)} %param.6) | copy-start | bytes 786436
  7.2 3.5 %copy-start.8 = (s32[8,8]{1,0:T(8,128)S(1)}, s32[8,8]{1,0:T(8,128)}, u32[]{:S(2)}) copy-start(s32[8,8]{1,0:T(8,128)} %param.9) | copy-start | bytes 772
  7.2 3.5 %copy-start.9 = (f32[8,128]{1,0:T(8,128)S(1)}, f32[8,128]{1,0:T(8,128)}, u32[]{:S(2)}) copy-start(f32[8,128]{1,0:T(8,128)} %param.10) | copy-start | bytes 12292
  7.2 3.6 %copy-start.7 = (bf16[8,128,128]{2,1,0:T(8,128)(2,1)S(1)}, bf16[8,128,128]{2,1,0:T(8,128)(2,1)}, u32[]{:S(2)}) copy-start(bf16[8,128,128]{2,1,0:T(8,128)(2,1)} %param.11) | copy-start | bytes 786436
  7.2 120.2 %all-gather.12.cloned.1.call-start = ((), (), s32[]{:S(2)}) async-start(), calls=%async_computation.6 | async-start | bytes 20054016 | tf_op jit(solution)/shard_map/all_gather | solution.py:400
  12.3 32.0 %all-to-all-start = ((f32[8,144,128]{2,1,0:T(8,128)}), f32[8,144,128]{2,1,0:T(8,128)S(1)}, u32[]{:S(2)}, u32[]{:S(2)}) async-start(f32[8,144,128]{2,1,0:T(8,128)} %pad_maximum_fusion.1), calls=%async_computation | async-start | bytes 1179648 | tf_op jit(solution)/shard_map/all_to_all | solution.py:415
  20.8 158.4 %all-gather.10.cloned.1.call-start = ((), (), s32[]{:S(2)}) async-start(), calls=%async_computation.5 | async-start | bytes 2228224 | tf_op jit(solution)/shard_map/all_gather | solution.py:434
  140.6 2.0 copy-start.3
  142.7 0.7 copy-start.5
  179.2 1.6 copy-start.1
  180.8 0.9 copy-start.6
  181.8 28.6 %copy-start.4 = (bf16[1024,16,128]{2,1,0:T(8,128)(2,1)S(1)}, bf16[1024,16,128]{2,1,0:T(8,128)(2,1)}, u32[]{:S(2)}) copy-start(bf16[1024,16,128]{2,1,0:T(8,128)(2,1)} %copy-done.3) | copy-start | bytes 12582916
  223.9 29.3 %copy-start.2 = (bf16[64,128,128]{2,1,0:T(8,128)(2,1)S(1)}, bf16[64,128,128]{2,1,0:T(8,128)(2,1)}, u32[]{:S(2)}) copy-start(bf16[64,128,128]{2,1,0:T(8,128)(2,1)} %all-gather.10.cloned.1.call-done.refs_7_) | copy-start | bytes 6291460
Sparse Core Ops, SparseCore 0:
  10.8 116.5 all-gather.11
  129.8 38.5 all-gather.9
where the time goes:
time: 344 us; the launch traced here: 343 us
  blocking collectives  182 us (53%)
  waiting for transfers between devices  77.4 us (23%)
  Pallas kernels  49.9 us (15%)
  between operations  14.3 us (4%)
  starting transfers between devices  8.54 us (2%)
  local copies, waits for them, and re-layouts  6.18 us (2%)
  other arithmetic  4.32 us (1%)
    all_to_all x3, blocking collectives, local(): lax.all_to_all(leaving, ('x', 'y'), split_axis=0, concat_axis=0, tiled=True)  88.1 us
    all_gather x3, blocking collectives, local(): arrived = lax.all_gather(codes, ('x', 'y'), axis=0, tiled=False)  78.8 us
    all_gather x1, waiting for transfers between devices, local(): tiles = lax.all_gather(mine, ('z', 'c'), axis=0, tiled=False)  54.6 us
    pallas_call x3, Pallas kernels, factor_call(): pl.pallas_call(lambda *refs: factor_kernel(first, last, peers, *refs), ou...  40.3 us
    all_to_all x1, waiting for transfers between devices, local(): came = lax.all_to_all(sent, 'z', split_axis=0, concat_axis=0, tiled=True)  22.8 us
    all_to_all x1, blocking collectives, local(): lax.all_to_all(results[0], 'z', split_axis=0, concat_axis=0, tiled=True)  15.2 us
    pallas_call x3, Pallas kernels, update_call(): pl.pallas_call(lambda *refs: update_kernel(last, codes.shape[0], *refs),...  8.61 us
    all_to_all x1, starting transfers between devices, local(): came = lax.all_to_all(sent, 'z', split_axis=0, concat_axis=0, tiled=True)  8.46 us
  transfers between devices with their start and end apart: 3, of which 2 were waited for; matrix products, arithmetic and copies ran while one was open for 1% of the time, Pallas kernels for 4%

commit v1 on v0

--- a/solution.py
+++ b/solution.py
@@ -11,7 +11,7 @@
 LANES = 128
 COLS = 8
 SHARE = 8
-GROUPS = 3
+GROUPS = 1
 EXTRA = (GROUPS + 1) * COLS
 BUFFERS = 8
 LOW_EXP = -100.0

time: 344 us -> 340 us (0.988)
  no operation moved by 1% of the time
where the time goes in v1:
time: 340 us
  blocking collectives  180 us (53%)
  waiting for transfers between devices  77.5 us (23%)
  Pallas kernels  49.8 us (15%)
  between operations  14.3 us (4%)
  starting transfers between devices  8.54 us (3%)
  local copies, waits for them, and re-layouts  4.52 us (1%)
  other arithmetic  4.31 us (1%)
    all_to_all x3, blocking collectives, local(): lax.all_to_all(leaving, ('x', 'y'), split_axis=0, concat_axis=0, tiled=True)  86.7 us
    all_gather x3, blocking collectives, local(): arrived = lax.all_gather(codes, ('x', 'y'), axis=0, tiled=False)  78.2 us
    all_gather x1, waiting for transfers between devices, local(): tiles = lax.all_gather(mine, ('z', 'c'), axis=0, tiled=False)  54.6 us
    pallas_call x3, Pallas kernels, factor_call(): pl.pallas_call(lambda *refs: factor_kernel(first, last, peers, *refs), ou...  40.2 us
    all_to_all x1, waiting for transfers between devices, local(): came = lax.all_to_all(sent, 'z', split_axis=0, concat_axis=0, tiled=True)  22.8 us
    all_to_all x1, blocking collectives, local(): lax.all_to_all(results[0], 'z', split_axis=0, concat_axis=0, tiled=True)  15.2 us
    pallas_call x3, Pallas kernels, update_call(): pl.pallas_call(lambda *refs: update_kernel(last, codes.shape[0], *refs),...  8.59 us
    all_to_all x1, starting transfers between devices, local(): came = lax.all_to_all(sent, 'z', split_axis=0, concat_axis=0, tiled=True)  8.46 us
  transfers between devices with their start and end apart: 3, of which 2 were waited for; matrix products, arithmetic and copies ran while one was open for 1% of the time, Pallas kernels for 4%

profile of v1, /device:TPU:2, one launch (start us, length us, event | category | flops | bytes accessed | tf_op | source)
XLA Modules:
  0.0 339.6 jit_solution(4472399936968822959)
XLA Ops:
  7.2 0.0 copy-start
  7.2 0.0 copy-start.6
  7.2 0.0 copy-start.7
  7.2 0.0 copy-start.5
  7.2 0.0 all-gather.12.cloned.1.call-start
  7.3 1.1 slice_select_fusion
  8.3 2.4 pad_maximum_fusion
  10.7 0.0 all-gather.12.cloned.1.call-update
  10.7 0.0 copy-done.6
  10.7 0.0 copy-done.7
  10.8 0.0 copy-done
  10.8 0.0 copy-done.5
  10.8 0.6 convolution_bitcast_fusion
  11.5 0.9 pad_maximum_fusion.1
  12.3 8.5 %all-to-all-start = ((f32[8,144,128]{2,1,0:T(8,128)}), f32[8,144,128]{2,1,0:T(8,128)S(1)}, u32[]{:S(2)}, u32[]{:S(2)}) async-start(f32[8,144,128]{2,1,0:T(8,128)} %pad_maximum_fusion.1), calls=%async_computation | async-start | bytes 1179648 | tf_op jit(solution)/shard_map/all_to_all | solution.py:415
  20.8 0.0 all-gather.10.cloned.1.call-start
  20.8 0.7 constant_dynamic-slice_fusion
  21.5 22.8 %all-to-all-done = f32[8,144,128]{2,1,0:T(8,128)S(1)} async-done(((f32[8,144,128]{2,1,0:T(8,128)}), f32[8,144,128]{2,1,0:T(8,128)S(1)}, u32[]{:S(2)}, u32[]{:S(2)}) %all-to-all-start) | async-done | bytes 589856 | tf_op jit(solution)/shard_map/all_to_all | solution.py:415
  44.3 0.1 reshape.45
  44.5 0.2 start.1
  44.7 28.1 %all-gather.13 = s16[8448,128]{1,0:T(8,128)(2,1)S(1)} all-gather(s16[528,128]{1,0:T(8,128)(2,1)S(1)} %start.1), channel_id=2, replica_groups=mesh['z'=8,'x'=4,'y'=4,'c'=2] {'x','y'}, dimensions={0}, use_global_device_ids=true | all-gather | bytes 2297856 | tf_op jit(solution)/shard_map/all_gather | solution.py:429
  72.8 54.6 %all-gather.12.cloned.1.call-done = bf16[576,128,128]{2,1,0:T(8,128)(2,1)} async-done(((bf16[36,128,128]{2,1,0:T(8,128)(2,1)}), bf16[576,128,128]{2,1,0:T(8,128)(2,1)}) %all-gather.12.cloned.1.call-update) | async-done | bytes 18874384 | tf_op jit(solution)/shard_map/all_gather | solution.py:400
  127.4 0.0 all-gather.10.cloned.1.call-update
  127.4 13.2 %factor.3 = (s16[16,528,128]{2,1,0:T(8,128)(2,1)S(1)}, f32[64,8,128]{2,1,0:T(8,128)S(1)}, f32[64,8,128]{2,1,0:T(8,128)S(1)}, f32[8,128]{1,0:T(8,128)S(1)}, bf16[1024,16,128]{2,1,0:T(8,128)(2,1)S(1)}) custom-call(s32[512]{0:T(512)S(1)} %fusion.3.refs_0_, s32[1]{0:T(128)} %bitcast.refs_1_.refs_0_, s16[16,528,128]{2,1,0:T(8,128)(2,1)S(1)} %bitcast.25, ...), custom_call_target="tpu_custom_call" | custom-call | tf_op jit(solution)/shard_map/factor/pallas_call | solution.py:340
  140.6 0.0 copy-start.3
  140.6 2.0 copy-done.3
  142.7 35.3 %all_to_all.25.refs_1_ = s16[16,528,128]{2,1,0:T(8,128)(2,1)S(1)} all-to-all(s16[16,528,128]{2,1,0:T(8,128)(2,1)S(1)} %get-tuple-element.33), channel_id=1, replica_groups=mesh['z'=8,'x'=4,'y'=4,'c'=2] {'x','y'}, dimensions={0} | all-to-all | bytes 4325376 | tf_op jit(solution)/shard_map/all_to_all | solution.py:438
  178.0 0.0 all-gather.10.cloned.1.call-done.refs_7_
  178.0 0.0 copy-start.1
  178.0 1.6 copy-done.1
  179.6 0.0 copy-start.4
  179.6 3.1 update.3
  182.7 25.2 %all-gather.14 = s16[8448,128]{1,0:T(8,128)(2,1)S(1)} all-gather(s16[528,128]{1,0:T(8,128)(2,1)S(1)} %get-tuple-element.38), channel_id=4, replica_groups=mesh['z'=8,'x'=4,'y'=4,'c'=2] {'x','y'}, dimensions={0}, use_global_device_ids=true | all-gather | bytes 2297856 | tf_op jit(solution)/shard_map/all_gather | solution.py:429
  207.9 0.0 copy-done.4
  207.9 13.5 %factor.4 = (s16[16,528,128]{2,1,0:T(8,128)(2,1)S(1)}, f32[64,8,128]{2,1,0:T(8,128)S(1)}, f32[64,8,128]{2,1,0:T(8,128)S(1)}, f32[8,128]{1,0:T(8,128)S(1)}, bf16[1024,16,128]{2,1,0:T(8,128)(2,1)S(1)}) custom-call(s32[512]{0:T(512)S(1)} %fusion.3.refs_0_, s32[1]{0:T(128)} %bitcast.refs_1_.refs_0_, s16[16,528,128]{2,1,0:T(8,128)(2,1)S(1)} %bitcast.27, ...), custom_call_target="tpu_custom_call" | custom-call | tf_op jit(solution)/shard_map/factor/pallas_call | solution.py:340
  221.4 0.0 copy-start.2
  221.4 28.7 %all_to_all.26.refs_1_ = s16[16,528,128]{2,1,0:T(8,128)(2,1)S(1)} all-to-all(s16[16,528,128]{2,1,0:T(8,128)(2,1)S(1)} %get-tuple-element.41), channel_id=1, replica_groups=mesh['z'=8,'x'=4,'y'=4,'c'=2] {'x','y'}, dimensions={0} | all-to-all | bytes 4325376 | tf_op jit(solution)/shard_map/all_to_all | solution.py:438
  250.0 0.0 copy-done.2
  250.0 3.1 update.4
  253.1 25.0 %all-gather.15 = s16[8448,128]{1,0:T(8,128)(2,1)S(1)} all-gather(s16[528,128]{1,0:T(8,128)(2,1)S(1)} %get-tuple-element.47), channel_id=5, replica_groups=mesh['z'=8,'x'=4,'y'=4,'c'=2] {'x','y'}, dimensions={0}, use_global_device_ids=true | all-gather | bytes 2297856 | tf_op jit(solution)/shard_map/all_gather | solution.py:429
  278.1 13.5 %factor.5 = (s16[16,528,128]{2,1,0:T(8,128)(2,1)S(1)}, f32[64,8,128]{2,1,0:T(8,128)S(1)}, f32[64,8,128]{2,1,0:T(8,128)S(1)}, f32[8,128]{1,0:T(8,128)S(1)}) custom-call(s32[512]{0:T(512)S(1)} %fusion.3.refs_0_, s32[1]{0:T(128)} %bitcast.refs_1_.refs_0_, s16[16,528,128]{2,1,0:T(8,128)(2,1)S(1)} %bitcast.26, f32[64,8,128]{2,1,0:T(8,128)S(1)} %get-tuple-element.48.refs_3_, ...), custom_call_target="tpu_custom_call" | custom-call | tf_op jit(solution)/shard_map/factor/pallas_call | solution.py:340
  291.6 22.7 %all_to_all.27.refs_1_ = s16[16,528,128]{2,1,0:T(8,128)(2,1)S(1)} all-to-all(s16[16,528,128]{2,1,0:T(8,128)(2,1)S(1)} %get-tuple-element.50), channel_id=1, replica_groups=mesh['z'=8,'x'=4,'y'=4,'c'=2] {'x','y'}, dimensions={0} | all-to-all | bytes 4325376 | tf_op jit(solution)/shard_map/all_to_all | solution.py:438
  314.3 2.5 update.5
  316.7 15.2 %all_to_all.28.code_ref = s16[8,144,128]{2,1,0:T(8,128)(2,1)S(1)} all-to-all(s16[8,144,128]{2,1,0:T(8,128)(2,1)S(1)} %update.5), channel_id=1, replica_groups=mesh['z'=8,'x'=4,'y'=4,'c'=2] {'z'}, dimensions={0} | all-to-all | bytes 589824 | tf_op jit(solution)/shard_map/all_to_all | solution.py:446
  331.9 0.9 finish.1
  (9 shorter events, 0.2 us)
Async XLA Ops:
  7.2 3.6 %copy-start = (f32[8,64,128]{2,1,0:T(8,128)S(1)}, f32[8,64,128]{2,1,0:T(8,128)}, u32[]{:S(2)}) copy-start(f32[8,64,128]{2,1,0:T(8,128)} %param.6) | copy-start | bytes 786436
  7.2 3.5 %copy-start.6 = (s32[8,8]{1,0:T(8,128)S(1)}, s32[8,8]{1,0:T(8,128)}, u32[]{:S(2)}) copy-start(s32[8,8]{1,0:T(8,128)} %param.9) | copy-start | bytes 772
  7.2 3.5 %copy-start.7 = (f32[8,128]{1,0:T(8,128)S(1)}, f32[8,128]{1,0:T(8,128)}, u32[]{:S(2)}) copy-start(f32[8,128]{1,0:T(8,128)} %param.10) | copy-start | bytes 12292
  7.2 3.6 %copy-start.5 = (bf16[8,128,128]{2,1,0:T(8,128)(2,1)S(1)}, bf16[8,128,128]{2,1,0:T(8,128)(2,1)}, u32[]{:S(2)}) copy-start(bf16[8,128,128]{2,1,0:T(8,128)(2,1)} %param.11) | copy-start | bytes 786436
  7.2 120.2 %all-gather.12.cloned.1.call-start = ((), (), s32[]{:S(2)}) async-start(), calls=%async_computation.6 | async-start | bytes 20054016 | tf_op jit(solution)/shard_map/all_gather | solution.py:400
  12.3 32.0 %all-to-all-start = ((f32[8,144,128]{2,1,0:T(8,128)}), f32[8,144,128]{2,1,0:T(8,128)S(1)}, u32[]{:S(2)}, u32[]{:S(2)}) async-start(f32[8,144,128]{2,1,0:T(8,128)} %pad_maximum_fusion.1), calls=%async_computation | async-start | bytes 1179648 | tf_op jit(solution)/shard_map/all_to_all | solution.py:415
  20.8 157.2 %all-gather.10.cloned.1.call-start = ((), (), s32[]{:S(2)}) async-start(), calls=%async_computation.5 | async-start | bytes 2228224 | tf_op jit(solution)/shard_map/all_gather | solution.py:434
  140.6 2.0 copy-start.3
  178.0 1.6 copy-start.1
  179.6 28.2 %copy-start.4 = (bf16[1024,16,128]{2,1,0:T(8,128)(2,1)S(1)}, bf16[1024,16,128]{2,1,0:T(8,128)(2,1)}, u32[]{:S(2)}) copy-start(bf16[1024,16,128]{2,1,0:T(8,128)(2,1)} %copy-done.3) | copy-start | bytes 12582916
  221.4 28.7 %copy-start.2 = (bf16[64,128,128]{2,1,0:T(8,128)(2,1)S(1)}, bf16[64,128,128]{2,1,0:T(8,128)(2,1)}, u32[]{:S(2)}) copy-start(bf16[64,128,128]{2,1,0:T(8,128)(2,1)} %all-gather.10.cloned.1.call-done.refs_7_) | copy-start | bytes 6291460
Sparse Core Ops, SparseCore 0:
  10.8 116.5 all-gather.11
  129.8 38.5 all-gather.9
